TPU v7x, 768 devices: a whole 4x8x12 slice. The times are simulated.
768 devices in a mesh: ctx: 96 (over z, y_hi, core), ch: 8 (over y_lo, x).
Axes of the slice: x: 4, y: 8 (y_hi: 4, y_lo: 2; y = y_hi * 2 + y_lo), z: 12, core: 2. Of those that a mesh axis runs over, the one named last changes fastest.
Arguments:
- features: bfloat16 [3, 24576, 8192], P(None, 'ctx', 'ch'), may hold values from -6 to 6
- short_filter: float32 [3, 7, 8192], P(None, None, 'ch'), may hold values from -4 to 4
- long_filter: float32 [512, 128], P('ch'), may hold values from -0.5 to 0.5
- cotangent: bfloat16 [24576, 8192], P('ctx', 'ch'), may hold values from -15 to 15
Outputs:
- grad_features: bfloat16 [3, 24576, 8192], P(None, 'ctx', 'ch')
- grad_short: float32 [3, 7, 8192], P(None, None, 'ch')
- grad_long: float32 [512, 128], P('ch')
All inputs are finite; a program needn't handle non-finite values.
Results may differ from a plain program's by a relative error of at most 0.0057.
Values may be sent and summed in bfloat16 or wider, within the bound.
A program may use at most 128 MiB of HBM per device.

v0:
```python
import jax
import jax.numpy as jnp
from jax import lax
from jax.sharding import PartitionSpec as P

D = 8192
G = 512


def from_behind(block, axis, distance):
    devices = range(lax.axis_size(axis))
    route = [(i - distance, i) for i in devices if i - distance in devices]
    return lax.ppermute(block, axis, route)


def short_conv(extended, filt, count):
    taps = filt.shape[0]
    total = jnp.zeros((count, extended.shape[1]), jnp.float32)
    for tap in range(taps):
        start = taps - 1 - tap
        total = total + filt[tap] * extended[start : start + count].astype(jnp.float32)
    return total


def short_adjoint(grad, filt):
    taps = filt.shape[0]
    count = grad.shape[0]
    edge = jnp.zeros((taps - 1, grad.shape[1]), jnp.float32)
    padded = jnp.concatenate([edge, grad, edge], 0)
    total = jnp.zeros((count + taps - 1, grad.shape[1]), jnp.float32)
    for tap in range(taps):
        total = total + filt[tap] * padded[tap : tap + count + taps - 1]
    return total


def filter_grad(grad, extended, taps):
    count = grad.shape[0]
    pieces = []
    for tap in range(taps):
        start = taps - 1 - tap
        pieces.append(jnp.sum(grad * extended[start : start + count].astype(jnp.float32), 0))
    return jnp.stack(pieces)


def toeplitz(long_filter):
    groups, span = long_filter.shape
    rounded = long_filter.astype(jnp.bfloat16)
    line = jnp.concatenate(
        [
            jnp.zeros((groups, 1), jnp.bfloat16),
            rounded[:, ::-1],
            jnp.zeros((groups, 2 * span - 1), jnp.bfloat16),
        ],
        1,
    )
    flat = jnp.tile(line, (1, span))[:, : span * (3 * span - 1)]
    return flat.reshape(groups, span, 3 * span - 1)[:, :, : 2 * span]


def time_last(values, groups, span):
    count = values.shape[0] // span
    width = values.shape[1]
    turned = jnp.transpose(values.reshape(count, span, width), (0, 2, 1))
    return turned.reshape(count, groups, width // groups, span)


def time_first(blocked):
    count, groups, members, span = blocked.shape
    turned = jnp.transpose(blocked.reshape(count, groups * members, span), (0, 2, 1))
    return turned.reshape(count * span, groups * members)


def long_forward(z_pad, matrix, groups, span):
    blocks = time_last(z_pad, groups, span)
    lower = jnp.einsum(
        "bgcs,gts->bgct", blocks[:-1], matrix[:, :, :span], preferred_element_type=jnp.float32
    )
    upper = jnp.einsum(
        "bgcs,gts->bgct", blocks[1:], matrix[:, :, span:], preferred_element_type=jnp.float32
    )
    return time_first(lower + upper)


def long_adjoint(grad_y, matrix, groups, span):
    blocks = time_last(grad_y, groups, span)
    lower = jnp.einsum(
        "bgct,gts->bgcs", blocks, matrix[:, :, :span], preferred_element_type=jnp.float32
    )
    upper = jnp.einsum(
        "bgct,gts->bgcs", blocks, matrix[:, :, span:], preferred_element_type=jnp.float32
    )
    zero = jnp.zeros((1,) + lower.shape[1:], jnp.float32)
    total = jnp.concatenate([lower, zero], 0) + jnp.concatenate([zero, upper], 0)
    return time_first(total)


def long_filter_grad(grad_y, z_pad, groups, span):
    blocks = time_last(grad_y, groups, span)
    z_blocks = time_last(z_pad, groups, span)
    lower = jnp.einsum("bgct,bgcs->gts", blocks, z_blocks[:-1], preferred_element_type=jnp.float32)
    upper = jnp.einsum("bgct,bgcs->gts", blocks, z_blocks[1:], preferred_element_type=jnp.float32)
    inner = jnp.concatenate([lower, upper], 2)
    flat = jnp.concatenate(
        [inner.reshape(groups, span * 2 * span), jnp.zeros((groups, span), jnp.float32)], 1
    )
    skewed = flat.reshape(groups, span, 2 * span + 1)
    columns = jnp.sum(skewed, 1)
    return columns[:, 1 : span + 1][:, ::-1]


def add_tail(own, later):
    cut = own.shape[0] - later.shape[0]
    return jnp.concatenate([own[:cut], own[cut:] + later], 0)


def on_device(features, short_filter, long_filter, cotangent):
    rows = features.shape[1]
    width = features.shape[2]
    taps = short_filter.shape[1]
    groups, span = long_filter.shape
    reach = span + taps - 2
    earlier = from_behind(features[:, rows - reach :], "ctx", 1)
    q_prior = earlier[0, reach - (taps - 1) :]
    kv_prior = earlier[1:]
    q_ext = jnp.concatenate([q_prior, features[0]], 0)
    k_ext = jnp.concatenate([kv_prior[0], features[1]], 0)
    v_ext = jnp.concatenate([kv_prior[1], features[2]], 0)
    q_short = short_conv(q_ext, short_filter[0], rows)
    k_short = short_conv(k_ext, short_filter[1], rows + span - 1)
    v_short = short_conv(v_ext, short_filter[2], rows + span - 1)
    gated = (k_short * v_short).astype(jnp.bfloat16)
    z_pad = jnp.concatenate([jnp.zeros((1, width), jnp.bfloat16), gated], 0)
    matrix = toeplitz(long_filter)
    y_long = long_forward(z_pad, matrix, groups, span)
    cot = cotangent.astype(jnp.float32)
    grad_y = (cot * q_short).astype(jnp.bfloat16)
    grad_q_short = cot * y_long
    raw_long = long_filter_grad(grad_y, z_pad, groups, span)
    raw_q = filter_grad(grad_q_short, q_ext, taps)
    grad_z = long_adjoint(grad_y, matrix, groups, span)[1:]
    grad_k_short = grad_z * v_short
    grad_v_short = grad_z * k_short
    k_part = short_adjoint(grad_k_short, short_filter[1])
    v_part = short_adjoint(grad_v_short, short_filter[2])
    q_part = short_adjoint(grad_q_short, short_filter[0])
    raw_k = filter_grad(grad_k_short, k_ext, taps)
    raw_v = filter_grad(grad_v_short, v_ext, taps)
    later_kv, later_q = (
        from_behind(
            jnp.stack([k_part[:reach], v_part[:reach]]).astype(jnp.bfloat16), "ctx", -1
        ).astype(jnp.float32),
        from_behind(q_part[: taps - 1].astype(jnp.bfloat16), "ctx", -1).astype(jnp.float32),
    )
    grad_q = add_tail(q_part[taps - 1 :], later_q)
    grad_k = add_tail(k_part[reach:], later_kv[0])
    grad_v = add_tail(v_part[reach:], later_kv[1])
    raw_short = jnp.stack([raw_q, raw_k, raw_v])
    raw_short, raw_long = lax.psum((raw_short, raw_long), "ctx")
    local_square = jnp.sum(raw_short * raw_short) + jnp.sum(raw_long * raw_long)
    total_square = lax.psum(local_square, "ch")
    mean_square = total_square / (3 * taps * D + span * G)
    factor = lax.rsqrt(mean_square + 1e-06)
    grads = jnp.stack([grad_q, grad_k, grad_v]).astype(jnp.bfloat16)
    return (grads, raw_short * factor, raw_long * factor)


def solution(mesh):
    in_specs = (P(None, "ctx", "ch"), P(None, None, "ch"), P("ch", None), P("ctx", "ch"))
    out_specs = (P(None, "ctx", "ch"), P(None, None, "ch"), P("ch", None))
    return jax.shard_map(
        on_device, mesh=mesh, in_specs=in_specs, out_specs=out_specs, check_vma=False
    )
```

profile of v0, /device:TPU:1, one launch (start us, length us, event | category | flops | bytes accessed | tf_op | source)
XLA Modules:
  0.0 847.5 jit_solution(11577649925930596198)
XLA Ops:
  7.2 1.4 slice.379
  8.6 5.6 collective-permute-start
  14.5 0.5 tile.4
  15.1 4.1 copy.46
  19.1 3.1 slice.458
  22.3 16.6 %reshape.89 = bf16[64,128,383]{2,1,0:T(8,128)(2,1)} reshape(bf16[64,49024]{1,0:T(8,128)(2,1)} %slice.458) | data formatting | bytes 12550144 | tf_op jit(solution)/shard_map/reshape | solution.py:57
  39.0 1.1 slice_bitcast_fusion.18
  40.1 1.0 fusion.52
  41.4 2.4 fusion.42
  43.8 2.2 fusion.43
  46.9 1.5 slice_bitcast_fusion.22
  48.4 7.2 fusion.41
  55.6 4.6 fusion.28
  60.7 1.1 fusion.100
  61.8 2.1 copy.32
  63.9 2.1 copy.30
  65.9 2.9 fusion.13
  68.9 2.8 fusion.45
  71.7 1.1 copy.34
  72.7 2.5 copy.35
  75.3 4.1 fusion.65
  79.5 1.9 fusion.94
  81.4 1.0 slice.494
  82.9 2.5 fusion.96
  85.4 1.3 fusion.98
  86.8 0.8 slice.524
  88.1 2.7 convolution_bitcast_fusion
  90.8 2.8 convolution_bitcast_fusion.1
  93.8 0.7 pad_maximum_fusion.11
  94.5 8.2 collective-permute-start.1
  102.7 1.4 copy.41
  104.1 1.9 collective-permute-start.2
  106.0 7.7 pad_maximum_fusion
  113.8 9.2 %copy.47 = f32[8,8,128,256]{3,1,2,0:T(8,128)} copy(f32[8,8,128,256]{2,3,1,0:T(8,128)} %bitcast.141) | data formatting | bytes 16777216
  122.9 7.3 concatenate.86
  130.2 14.2 %reshape.98 = f32[64,128,257]{2,1,0:T(8,128)} reshape(f32[64,32896]{1,0:T(8,128)} %concatenate.86) | data formatting | bytes 16842752 | tf_op jit(solution)/shard_map/reshape | solution.py:106
  144.4 6.2 reduce_sum.238
  150.7 416.7 %psum.22 = f32[64,128]{1,0:T(8,128)S(1)} all-reduce(f32[64,128]{1,0:T(8,128)S(1)} %rev.7), channel_id=1, replica_groups=mesh['ctx'=96,'ch'=8] {'ctx'}, use_global_device_ids=true, to_apply=%region_24.0 | all-reduce | flops 8192 | bytes 65536 | tf_op jit(solution)/shard_map/psum | solution.py:158
  567.4 0.6 multiply_reduce_fusion.1
  568.0 0.8 fusion.91
  568.8 247.6 %all-reduce.12.cloned.1.call-done = f32[3,7,1024]{2,1,0:T(8,128)} async-done(((f32[3,7,1024]{2,1,0:T(8,128)}), f32[3,7,1024]{2,1,0:T(8,128)}) %all-reduce.12.cloned.1.call-update) | async-done | bytes 86032 | tf_op jit(solution)/shard_map/psum | solution.py:158
  816.4 1.5 multiply_reduce_fusion
  819.3 14.6 %psum.23 = f32[]{:T(128)} all-reduce(f32[]{:T(128)S(6)} %add.200), channel_id=1, replica_groups=mesh['ctx'=96,'ch'=8] {'ch'}, use_global_device_ids=true, to_apply=%region_26.0 | all-reduce | flops 1 | bytes 8 | tf_op jit(solution)/shard_map/psum | solution.py:160
  834.6 0.6 broadcast_multiply_fusion.1
  835.2 1.5 broadcast_multiply_fusion
  836.7 1.2 copy_convert_fusion
  838.0 1.2 fusion.81
  839.4 1.3 pad_maximum_fusion.5
  (75 shorter events, 3.8 us)
Async XLA Ops:
  7.2 7.1 copy-start.15
  7.2 809.3 %all-reduce.12.cloned.1.call-start = ((), (), s32[]{:S(2)}) async-start(), calls=%async_computation | async-start | bytes 196608 | tf_op jit(solution)/shard_map/psum | solution.py:158
  8.6 31.5 %collective-permute-start = (bf16[3,133,1024]{2,1,0:T(8,128)(2,1)S(1)}, bf16[3,133,1024]{2,1,0:T(8,128)(2,1)S(1)}, u32[]{:S(2)}, u32[]{:S(2)}) collective-permute-start(bf16[3,133,1024]{2,1,0:T(8,128)(2,1)S(1)} %slice.379), channel_id=1, source_target_pairs={{0,8},{8,16},{16,24},{24,32},{32,40},{40,48},{48,56},{56,64},{64,7... | collective-permute-start | bytes 2451464 | tf_op jit(solution)/shard_map/ppermute | solution.py:13
  22.3 16.6 %copy-start.14 = (f32[3,7,1024]{2,1,0:T(8,128)S(1)}, f32[3,7,1024]{2,1,0:T(8,128)}, u32[]{:S(2)}) copy-start(f32[3,7,1024]{2,1,0:T(8,128)} %param.5) | copy-start | bytes 258052
  22.3 16.7 %copy-start.3 = (bf16[3,256,1024]{2,1,0:T(8,128)(2,1)S(1)}, bf16[3,256,1024]{2,1,0:T(8,128)(2,1)}, u32[]{:S(2)}) copy-start(bf16[3,256,1024]{2,1,0:T(8,128)(2,1)} %param.4) | copy-start | bytes 4718596
  39.0 1.1 copy-start.10
  40.1 1.0 copy-start.9
  40.1 3.8 copy-start.13
  41.4 2.4 copy-start.1
  46.9 8.7 %copy-start = (f32[3,128,1024]{2,1,0:T(8,128)}, f32[3,128,1024]{2,1,0:T(8,128)S(1)}, u32[]{:S(2)}) copy-start(f32[3,128,1024]{2,1,0:T(8,128)S(1)} %copy.40) | copy-start | bytes 4718596
  48.3 7.2 copy-start.7
  48.4 7.2 copy-start.8
  65.9 2.9 copy-start.4
  86.8 1.1 copy-start.2
  86.8 1.3 copy-start.5
  88.1 2.7 copy-start.6
  90.8 2.9 copy-start.16
  90.8 2.9 copy-start.17
  90.8 3.0 copy-start.18
  90.8 3.0 copy-start.19
  94.5 473.5 %collective-permute-start.1 = (bf16[6,1024]{1,0:T(8,128)(2,1)S(1)}, bf16[6,1024]{1,0:T(8,128)(2,1)S(1)}, u32[]{:S(2)}, u32[]{:S(2)}) collective-permute-start(bf16[6,1024]{1,0:T(8,128)(2,1)S(1)} %slice.496), channel_id=1, source_target_pairs={{8,0},{16,8},{24,16},{32,24},{40,32},{48,40},{56,48},{64,56},{72,6... | collective-permute-start | bytes 36872 | tf_op jit(solution)/shard_map/ppermute | solution.py:13
  104.1 732.6 %collective-permute-start.2 = (bf16[2,133,1024]{2,0,1:T(2,128)(2,1)}, bf16[2,133,1024]{2,0,1:T(2,128)(2,1)}, u32[]{:S(2)}, u32[]{:S(2)}) collective-permute-start(bf16[2,133,1024]{2,0,1:T(2,128)(2,1)} %copy.41), channel_id=1, source_target_pairs={{8,0},{16,8},{24,16},{32,24},{40,32},{48,40},{56,48},{64,56},{72,6... | collective-permute-start | bytes 1634312 | tf_op jit(solution)/shard_map/ppermute | solution.py:13
  144.4 674.9 %copy-start.11 = (bf16[250,1024]{1,0:T(8,128)(2,1)S(1)}, bf16[250,1024]{1,0:T(8,128)(2,1)}, u32[]{:S(2)}) copy-start(bf16[250,1024]{1,0:T(8,128)(2,1)} %slice.494) | copy-start | bytes 1536004
  837.9 1.3 copy-start.12
Sparse Core Ops, SparseCore 0:
  94.6 721.7 all-reduce.11
where the time goes:
time: 853 us; the launch traced here: 848 us
  blocking collectives  431 us (51%)
  waiting for transfers between devices  248 us (29%)
  local copies, waits for them, and re-layouts  73.1 us (9%)
  other arithmetic  47.4 us (6%)
  between operations  16.4 us (2%)
  matrix products  15.9 us (2%)
  starting transfers between devices  15.7 us (2%)
    psum x1, blocking collectives, on_device(): raw_short, raw_long = lax.psum((raw_short, raw_long), 'ctx')  417 us
    psum x1, waiting for transfers between devices, on_device(): raw_short, raw_long = lax.psum((raw_short, raw_long), 'ctx')  248 us
  transfers between devices with their start and end apart: 4, of which 1 were waited for; matrix products, arithmetic and copies ran while one was open for 9% of the time, Pallas kernels for 0%

commit v1 on v0

v1 whole, which is shorter than its diff:
```python
import jax
import jax.numpy as jnp
from jax import lax
from jax.experimental import pallas as pl
from jax.experimental.pallas import tpu as pltpu
from jax.sharding import PartitionSpec as P

MESH = pl.DeviceIdType.MESH
F32 = jnp.float32
BF16 = jnp.bfloat16

ROWS = 256
SPAN = 128
LANES = 128
TILES = 8
PLANES = 12
CH = 8
GROUP = 16
PER = LANES // GROUP
TAPS = 7
HEAD = 8
COUNT = 237568


def kernel(
    feat, sf, lf, cot, out_grads, out_short, out_long,
    xf, ks, vs, zw, dyw, fwd, bwd, dd, amat, bmat, hrev, gout,
    rawb, scat, gath, fin, sq,
    fwd_s, fwd_r, bwd_s, bwd_r, dd_s, dd_r, rs_s, rs_r, z_s, z_r, ag_s, ag_r, ch_s, ch_r, out_s,
):
    me = lax.axis_index("ctx")
    mc = lax.axis_index("ch")
    last = PLANES * TILES - 1
    plane = me // TILES
    part = lax.rem(me, TILES)
    after = lax.rem(me + 1, PLANES * TILES)
    before = lax.rem(me + last, PLANES * TILES)

    def z_peer(d):
        return lax.rem(plane + d, PLANES)

    def p_peer(d):
        return lax.rem(part + d, TILES)

    def c_peer(d):
        return lax.rem(mc + d, CH)

    barrier = pltpu.get_barrier_semaphore()
    peers = [(before, mc), (after, mc)]
    peers += [(plane * TILES + p_peer(d), mc) for d in range(1, TILES)]
    peers += [(me, c_peer(d)) for d in range(1, CH)]
    peers += [(z_peer(d) * TILES + part, mc) for d in range(1, PLANES)]
    for peer in peers:
        pl.semaphore_signal(barrier, inc=1, device_id=peer, device_id_type=MESH)

    def lanes(tile):
        return pl.ds(pl.multiple_of(tile * LANES, LANES), LANES)

    def taps(which, tile, start, count):
        total = sf[which, 0:1, lanes(tile)] * xf[tile, which, pl.ds(HEAD + start, count), :]
        for j in range(1, TAPS):
            total += sf[which, j : j + 1, lanes(tile)] * xf[tile, which, pl.ds(HEAD + start - j, count), :]
        return total

    def remote(src, dst, send, recv, ctx, ch):
        return pltpu.make_async_remote_copy(
            src_ref=src, dst_ref=dst, send_sem=send, recv_sem=recv, device_id=(ctx, ch), device_id_type=MESH
        )

    def fwd_copy(tile):
        return remote(fwd.at[tile], zw.at[tile, pl.ds(0, 160)], fwd_s.at[tile], fwd_r.at[tile], after, mc)

    def bwd_copy(tile):
        return remote(bwd.at[tile], dyw.at[tile, pl.ds(ROWS, 144)], bwd_s.at[tile], bwd_r.at[tile], before, mc)

    def dd_copy(tile):
        return remote(
            dd.at[tile, :, pl.ds(0, 8)], dd.at[tile, :, pl.ds(ROWS, 8)], dd_s.at[tile], dd_r.at[tile], before, mc
        )

    def first(tile, _):
        zero8 = jnp.zeros((8, LANES), F32)
        for which in range(3):
            xf[tile, which, pl.ds(HEAD, ROWS), :] = feat[which, :, lanes(tile)].astype(F32)
        k_short = taps(1, tile, 8, ROWS - 8)
        ks[tile, pl.ds(8, ROWS - 8), :] = k_short
        v_short = taps(2, tile, 8, ROWS - 8)
        vs[tile, pl.ds(8, ROWS - 8), :] = v_short
        gated = jnp.concatenate([zero8, k_short * v_short], 0).astype(BF16)
        zw[tile, pl.ds(160, ROWS), :] = gated
        tails = [xf[tile, which, pl.ds(ROWS, 8), :] for which in range(3)] + [zero8]
        fwd[tile, pl.ds(0, 32), :] = jnp.concatenate(tails, 0).astype(BF16)
        fwd[tile, pl.ds(32, SPAN), :] = gated[SPAN:]

        cotf = cot[:, lanes(tile)].astype(F32)
        grad_y = jnp.concatenate([zero8, cotf[8:] * taps(0, tile, 8, ROWS - 8)], 0).astype(BF16)
        dyw[tile, pl.ds(0, ROWS), :] = grad_y
        bwd[tile, pl.ds(0, SPAN), :] = grad_y[:SPAN]
        bwd[tile, pl.ds(SPAN, 16), :] = jnp.concatenate(
            [xf[tile, 0, pl.ds(HEAD, 8), :], cotf[:8]], 0
        ).astype(BF16)

        @pl.when(tile == 0)
        def _():
            pl.semaphore_wait(barrier, len(peers))

        fwd_copy(tile).start()
        bwd_copy(tile).start()
        return 0

    lax.fori_loop(0, TILES, first, 0)

    row = lax.broadcasted_iota(jnp.int32, (SPAN, SPAN), 0)
    col = lax.broadcasted_iota(jnp.int32, (SPAN, SPAN), 1)
    flip = jnp.where(row + col == SPAN - 1, 1.0, 0.0).astype(BF16)
    hb = lf[...].astype(BF16)
    hrev[0] = hb.astype(F32)
    hrev[1] = jnp.dot(hb, flip, preferred_element_type=F32)

    def build(g, _):
        wide = [
            jnp.broadcast_to(
                jnp.concatenate([hrev[i, pl.ds(g, 1), :], jnp.zeros((1, SPAN), F32)], 1), (SPAN, 2 * SPAN)
            )
            for i in range(2)
        ]
        bmat[g] = pltpu.roll(wide[0], 0, axis=1, stride=1, stride_axis=0).astype(BF16)
        amat[g] = pltpu.roll(wide[1], 1, axis=1, stride=1, stride_axis=0).astype(BF16)
        return 0

    lax.fori_loop(0, TILES * PER, build, 0)

    lane = lax.rem(lax.broadcasted_iota(jnp.int32, (1, 2 * LANES), 1), LANES) // GROUP

    def pick(stacked):
        total = stacked[:SPAN]
        for g in range(1, PER):
            total = jnp.where(lane == g, stacked[g * SPAN : (g + 1) * SPAN], total)
        return total[:, :LANES], total[:, LANES:]

    def second(tile, _):
        fwd_copy(tile).wait_recv()
        bwd_copy(tile).wait_recv()

        @pl.when(me == 0)
        def _():
            zw[tile, pl.ds(0, 160), :] = jnp.zeros((160, LANES), BF16)

        @pl.when(me == last)
        def _():
            dyw[tile, pl.ds(ROWS, 144), :] = jnp.zeros((144, LANES), BF16)

        halo = zw[tile, pl.ds(0, 32), :].astype(F32)
        for which in range(3):
            xf[tile, which, pl.ds(0, HEAD), :] = halo[8 * which : 8 * which + 8]
        ahead = dyw[tile, pl.ds(ROWS + SPAN, 16), :].astype(F32)
        xf[tile, 0, pl.ds(HEAD + ROWS, 8), :] = ahead[:8]
        k_head = taps(1, tile, 0, 8)
        v_head = taps(2, tile, 0, 8)
        ks[tile, pl.ds(0, 8), :] = k_head
        vs[tile, pl.ds(0, 8), :] = v_head

        def patch(ref, start, value):
            old = ref[tile, pl.ds(start, 16), :].astype(F32)
            ref[tile, pl.ds(start, 16), :] = jnp.concatenate([value, old[8:]], 0).astype(BF16)

        cotf = cot[:, lanes(tile)].astype(F32)
        patch(zw, 160, k_head * v_head)
        patch(dyw, 0, cotf[:8] * taps(0, tile, 0, 8))
        patch(dyw, ROWS, ahead[8:] * taps(0, tile, ROWS, 8))

        z_win = jnp.concatenate([zw[tile, pl.ds(32, 256), :], zw[tile, pl.ds(160, 256), :]], 1)
        d_win = jnp.concatenate([dyw[tile, pl.ds(0, 256), :], dyw[tile, pl.ds(128, 256), :]], 1)
        groups = pl.ds(tile * PER, PER)
        y_all = jnp.dot(amat[groups].reshape(PER * SPAN, 2 * SPAN), z_win, preferred_element_type=F32)
        y0, y1 = pick(y_all)
        dd[tile, 0, pl.ds(0, SPAN), :] = cotf[:SPAN] * y0
        dd[tile, 0, pl.ds(SPAN, SPAN), :] = cotf[SPAN:] * y1
        g_all = jnp.dot(bmat[groups].reshape(PER * SPAN, 2 * SPAN), d_win, preferred_element_type=F32)
        for b, gz in enumerate(pick(g_all)):
            at = pl.ds(b * SPAN, SPAN)
            dd[tile, 1, at, :] = gz * vs[tile, at, :]
            dd[tile, 2, at, :] = gz * ks[tile, at, :]
        dd_copy(tile).start()

        z_own = jnp.concatenate([zw[tile, pl.ds(160, SPAN), :], zw[tile, pl.ds(160 + SPAN, SPAN), :]], 1)
        z_own = jnp.dot(flip, z_own, preferred_element_type=F32).astype(BF16)
        masked = jnp.concatenate([z_own * (lane == g).astype(BF16) for g in range(PER)], 0)
        gram = lax.dot_general(masked, d_win, (((1,), (1,)), ((), ())), preferred_element_type=F32)
        for g in range(PER):
            skew = pltpu.roll(
                gram[g * SPAN : (g + 1) * SPAN], SPAN + 1, axis=1, stride=1, stride_axis=0
            )
            rawb[tile, 24 + g : 25 + g, :] = jnp.sum(skew[:, :SPAN], 0, keepdims=True)
        for which in range(3):
            for j in range(TAPS):
                prod = dd[tile, which, pl.ds(0, ROWS), :] * xf[tile, which, pl.ds(HEAD - j, ROWS), :]
                rawb[tile, 8 * which + j : 8 * which + j + 1, :] = jnp.sum(prod, 0, keepdims=True)
            rawb[tile, 8 * which + 7 : 8 * which + 8, :] = jnp.zeros((1, LANES), F32)

        @pl.when(tile != part)
        def _():
            remote(
                rawb.at[tile], scat.at[part], rs_s.at[tile], rs_r.at[part], plane * TILES + tile, mc
            ).start()

        @pl.when(tile == part)
        def _():
            scat[part] = rawb[tile]

        return 0

    lax.fori_loop(0, TILES, second, 0)

    def out_copy(tile):
        return pltpu.make_async_copy(
            gout.at[:, :, lanes(tile)], out_grads.at[:, :, lanes(tile)], out_s.at[tile]
        )

    def adjoint(tile, _):
        dd_copy(tile).wait_recv()

        @pl.when(me == last)
        def _():
            dd[tile, :, pl.ds(ROWS, 8), :] = jnp.zeros((3, 8, LANES), F32)

        for which in range(3):
            total = sf[which, 0:1, lanes(tile)] * dd[tile, which, pl.ds(0, ROWS), :]
            for j in range(1, TAPS):
                total += sf[which, j : j + 1, lanes(tile)] * dd[tile, which, pl.ds(j, ROWS), :]
            gout[which, :, lanes(tile)] = total.astype(BF16)
        out_copy(tile).start()
        return 0

    lax.fori_loop(0, 3, adjoint, 0)

    def scat_wait(d, _):
        peer = p_peer(d)
        remote(rawb.at[peer], scat.at[peer], rs_s.at[peer], rs_r.at[peer], plane * TILES + peer, mc).wait()
        return 0

    lax.fori_loop(1, TILES, scat_wait, 0)
    gath[plane] = jnp.sum(scat[...], 0)

    def z_copy(peer, slot):
        return remote(
            gath.at[plane], gath.at[slot], z_s.at[peer], z_r.at[slot], peer * TILES + part, mc
        )

    def z_start(d, _):
        z_copy(z_peer(d), plane).start()
        return 0

    def z_wait(d, _):
        z_copy(z_peer(d), z_peer(d)).wait()
        return 0

    lax.fori_loop(1, PLANES, z_start, 0)
    lax.fori_loop(3, TILES, adjoint, 0)
    lax.fori_loop(1, PLANES, z_wait, 0)
    fin[part] = jnp.sum(gath[...], 0)

    def ag_copy(peer, slot):
        return remote(fin.at[part], fin.at[slot], ag_s.at[peer], ag_r.at[slot], plane * TILES + peer, mc)

    def ag_start(d, _):
        ag_copy(p_peer(d), part).start()
        return 0

    def ag_wait(d, _):
        ag_copy(p_peer(d), p_peer(d)).wait()
        return 0

    lax.fori_loop(1, TILES, ag_start, 0)
    lax.fori_loop(1, TILES, ag_wait, 0)
    whole = fin[...].reshape(TILES * 32 // 8, 8, LANES)
    sq[mc] = jnp.sum(whole * whole, 0)

    def ch_copy(peer, slot):
        return remote(sq.at[mc], sq.at[slot], ch_s.at[peer], ch_r.at[slot], me, peer)

    def ch_start(d, _):
        ch_copy(c_peer(d), mc).start()
        return 0

    def ch_wait(d, _):
        ch_copy(c_peer(d), c_peer(d)).wait()
        return 0

    lax.fori_loop(1, CH, ch_start, 0)
    lax.fori_loop(1, CH, ch_wait, 0)
    total = jnp.sum(sq[...], 0)
    total = jnp.sum(jnp.sum(total, 0, keepdims=True), 1, keepdims=True)
    factor = lax.rsqrt(total / COUNT + 1e-06)
    for tile in range(TILES):
        for which in range(3):
            out_short[which, :, tile * LANES : (tile + 1) * LANES] = (
                fin[tile, 8 * which : 8 * which + TAPS, :] * factor
            )
        out_long[8 * tile : 8 * tile + 8, :] = fin[tile, 24:32, :] * factor

    def drain(tile, _):
        fwd_copy(tile).wait_send()
        bwd_copy(tile).wait_send()
        dd_copy(tile).wait_send()
        out_copy(tile).wait()
        return 0

    lax.fori_loop(0, TILES, drain, 0)


def on_device(features, short_filter, long_filter, cotangent):
    vmem = pl.BlockSpec(memory_space=pltpu.VMEM)
    sems = [pltpu.SemaphoreType.DMA((n,)) for n in (8,) * 8 + (12, 12) + (8,) * 5]
    return pl.pallas_call(
        kernel,
        out_shape=(
            jax.ShapeDtypeStruct((3, ROWS, TILES * LANES), BF16),
            jax.ShapeDtypeStruct((3, TAPS, TILES * LANES), F32),
            jax.ShapeDtypeStruct((TILES * PER, SPAN), F32),
        ),
        in_specs=[vmem] * 4,
        out_specs=(pl.BlockSpec(memory_space=pl.ANY), vmem, vmem),
        scratch_shapes=[
            pltpu.VMEM((TILES, 3, HEAD + ROWS + 8, LANES), F32),
            pltpu.VMEM((TILES, ROWS, LANES), F32),
            pltpu.VMEM((TILES, ROWS, LANES), F32),
            pltpu.VMEM((TILES, 416, LANES), BF16),
            pltpu.VMEM((TILES, 400, LANES), BF16),
            pltpu.VMEM((TILES, 160, LANES), BF16),
            pltpu.VMEM((TILES, 144, LANES), BF16),
            pltpu.VMEM((TILES, 3, ROWS + 8, LANES), F32),
            pltpu.VMEM((TILES * PER, SPAN, 2 * SPAN), BF16),
            pltpu.VMEM((TILES * PER, SPAN, 2 * SPAN), BF16),
            pltpu.VMEM((2, TILES * PER, SPAN), F32),
            pltpu.VMEM((3, ROWS, TILES * LANES), BF16),
            pltpu.VMEM((TILES, 32, LANES), F32),
            pltpu.VMEM((TILES, 32, LANES), F32),
            pltpu.VMEM((PLANES, 32, LANES), F32),
            pltpu.VMEM((TILES, 32, LANES), F32),
            pltpu.VMEM((CH, 8, LANES), F32),
            *sems,
        ],
        compiler_params=pltpu.CompilerParams(
            collective_id=0, has_side_effects=True, vmem_limit_bytes=48 * 1024 * 1024
        ),
    )(features, short_filter, long_filter, cotangent)


def solution(mesh):
    in_specs = (P(None, "ctx", "ch"), P(None, None, "ch"), P("ch", None), P("ctx", "ch"))
    out_specs = (P(None, "ctx", "ch"), P(None, None, "ch"), P("ch", None))
    return jax.shard_map(
        on_device, mesh=mesh, in_specs=in_specs, out_specs=out_specs, check_vma=False
    )
```

time: 853 us -> 69.3 us (0.08)
  blocking collectives: 431 us -> 0 us
  waiting for transfers between devices: 248 us -> 0 us
  local copies, waits for them, and re-layouts: 73.1 us -> 6.49 us
  Pallas kernels: 0 us -> 61.8 us
  other arithmetic: 47.4 us -> 0 us
  matrix products: 15.9 us -> 0 us
  between operations: 16.4 us -> 0.65 us
  starting transfers between devices: 15.7 us -> 0 us
    psum x2 -> x0, blocking collectives: 431 us -> none  [the longest x1 417 us: on_device(): raw_short, raw_long = lax.psum((raw_short, raw_long), 'ctx')]
    psum x1 -> x0, waiting for transfers between devices: 248 us -> none  [on_device(): raw_short, raw_long = lax.psum((raw_short, raw_long), 'ctx')]
    pallas_call x0 -> x1, Pallas kernels: none -> 61.8 us  [on_device(): pl.pallas_call(kernel, out_shape=(jax.ShapeDtypeStruct((3, ROWS, TILES *...]
    reshape x2 -> x0, local copies, waits for them, and re-layouts: 30.8 us -> none  [the longest x1 16.6 us: toeplitz(): return flat.reshape(groups, span, 3 * span - 1)[:, :, :2 * span]]
    reduce_sum x6 -> x0, other arithmetic: 24.2 us -> none  [the longest x3 15.9 us: filter_grad(): jnp.sum(grad * extended[start:start + count].astype(jnp.float32), 0)]
    dot_general x6 -> x0, matrix products: 15.9 us -> none  [the longest x1 2.92 us: long_forward(): jnp.einsum('bgcs,gts->bgct', blocks[:-1], matrix[:, :, :span], preferred_...]
    ppermute x3 -> x0, starting transfers between devices: 15.7 us -> none  [from_behind(): return lax.ppermute(block, axis, route)]
    slice x12 -> x0, local copies, waits for them, and re-layouts: 11.6 us -> none  [the longest x2 3.15 us: long_forward(): blocks[1:]]
  transfers between devices with their start and end apart: 4 -> 0, of which waited for: 1 -> 0; matrix products, arithmetic and copies ran while one was open for 9% -> 0% of each run, Pallas kernels for 0% -> 0%
where the time goes in v1:
time: 69.3 us; the launch traced here: 69 us
  Pallas kernels  61.8 us (89%)
  local copies, waits for them, and re-layouts  6.49 us (9%)
    pallas_call x1, Pallas kernels, on_device(): pl.pallas_call(kernel, out_shape=(jax.ShapeDtypeStruct((3, ROWS, TILES *...  61.8 us
    unnamed x11, local copies, waits for them, and re-layouts  6.49 us

profile of v1, /device:TPU:1, one launch (start us, length us, event | category | flops | bytes accessed | tf_op | source)
XLA Modules:
  0.0 69.0 jit_solution(16688685228152059448)
XLA Ops:
  0.6 0.0 copy-start
  0.6 1.4 %copy-done = bf16[3,256,1024]{2,1,0:T(8,128)(2,1)S(1)} copy-done((bf16[3,256,1024]{2,1,0:T(8,128)(2,1)S(1)}, bf16[3,256,1024]{2,1,0:T(8,128)(2,1)}, u32[]{:S(2)}) %copy-start) | copy-done | bytes 1572888
  2.0 0.0 copy-start.1
  2.0 1.0 %copy-done.1 = bf16[256,1024]{1,0:T(8,128)(2,1)S(1)} copy-done((bf16[256,1024]{1,0:T(8,128)(2,1)S(1)}, bf16[256,1024]{1,0:T(8,128)(2,1)}, u32[]{:S(2)}) %copy-start.1) | copy-done | bytes 524312
  3.1 0.0 copy-start.2
  3.1 0.9 %copy-done.2 = f32[3,7,1024]{2,1,0:T(8,128)S(1)} copy-done((f32[3,7,1024]{2,1,0:T(8,128)S(1)}, f32[3,7,1024]{2,1,0:T(8,128)}, u32[]{:S(2)}) %copy-start.2) | copy-done | bytes 86040
  4.0 0.0 copy-start.3
  4.0 0.8 %copy-done.3 = f32[64,128]{1,0:T(8,128)S(1)} copy-done((f32[64,128]{1,0:T(8,128)S(1)}, f32[64,128]{1,0:T(8,128)}, u32[]{:S(2)}) %copy-start.3) | copy-done | bytes 32792
  4.7 61.8 %shard_map.67 = (bf16[3,256,1024]{2,1,0:T(8,128)(2,1)S(1)}, f32[3,7,1024]{2,1,0:T(8,128)S(1)}, f32[64,128]{1,0:T(8,128)S(1)}) custom-call(bf16[3,256,1024]{2,1,0:T(8,128)(2,1)S(1)} %copy-done, f32[3,7,1024]{2,1,0:T(8,128)S(1)} %copy-done.2, f32[64,128]{1,0:T(8,128)S(1)} %copy-done.3, bf16[256,1024]{1,0:T(8,128)(2,1)S(1)} %copy-done.1), custom_call_target="tpu_custom_call" | custom-call | tf_op jit(solution)/shard_map/pallas_call | solution.py:315
  66.6 1.1 %copy.10 = bf16[3,256,1024]{2,1,0:T(8,128)(2,1)} copy(bf16[3,256,1024]{2,1,0:T(8,128)(2,1)S(1)} %get-tuple-element.6) | data formatting | bytes 3145728
  67.7 0.6 copy.11
  68.4 0.6 copy.12
Async XLA Ops:
  0.6 1.4 %copy-start = (bf16[3,256,1024]{2,1,0:T(8,128)(2,1)S(1)}, bf16[3,256,1024]{2,1,0:T(8,128)(2,1)}, u32[]{:S(2)}) copy-start(bf16[3,256,1024]{2,1,0:T(8,128)(2,1)} %feat.1) | copy-start | bytes 4718596
  2.0 1.0 %copy-start.1 = (bf16[256,1024]{1,0:T(8,128)(2,1)S(1)}, bf16[256,1024]{1,0:T(8,128)(2,1)}, u32[]{:S(2)}) copy-start(bf16[256,1024]{1,0:T(8,128)(2,1)} %cot.1) | copy-start | bytes 1572868
  3.1 0.9 %copy-start.2 = (f32[3,7,1024]{2,1,0:T(8,128)S(1)}, f32[3,7,1024]{2,1,0:T(8,128)}, u32[]{:S(2)}) copy-start(f32[3,7,1024]{2,1,0:T(8,128)} %sf.1) | copy-start | bytes 258052
  4.0 0.8 %copy-start.3 = (f32[64,128]{1,0:T(8,128)S(1)}, f32[64,128]{1,0:T(8,128)}, u32[]{:S(2)}) copy-start(f32[64,128]{1,0:T(8,128)} %lf.1) | copy-start | bytes 98308

commit v2 on v1

--- a/solution.py
+++ b/solution.py
@@ -14,6 +14,8 @@
 LANES = 128
 TILES = 8
 PLANES = 12
+PAIRS = 6
+MEMBERS = 16
 CH = 8
 GROUP = 16
 PER = LANES // GROUP
@@ -23,10 +25,10 @@
 
 
 def kernel(
-    feat, sf, lf, cot, out_grads, out_short, out_long,
-    xf, ks, vs, zw, dyw, fwd, bwd, dd, amat, bmat, hrev, gout,
-    rawb, scat, gath, fin, sq,
-    fwd_s, fwd_r, bwd_s, bwd_r, dd_s, dd_r, rs_s, rs_r, z_s, z_r, ag_s, ag_r, ch_s, ch_r, out_s,
+    feat_in, sf_in, lf_in, cot_in, out_grads, out_short, out_long,
+    feat, sf, lf, cot, xf, ks, vs, zw, dyw, fwd, bwd, dd, amat, bmat, hrev, gout,
+    rawb, scat, gath, fin, sq, part_sq,
+    fwd_s, fwd_r, bwd_s, bwd_r, dd_s, dd_r, rs_s, rs_r, z_s, z_r, ag_s, ag_r, ch_s, ch_r, sq_s, sq_r, out_s, in_s,
 ):
     me = lax.axis_index("ctx")
     mc = lax.axis_index("ch")
@@ -36,25 +38,43 @@
     after = lax.rem(me + 1, PLANES * TILES)
     before = lax.rem(me + last, PLANES * TILES)
 
+    pair = plane // 2
+    odd = lax.rem(plane, 2)
+    member = odd * TILES + part
+
     def z_peer(d):
-        return lax.rem(plane + d, PLANES)
+        return lax.rem(pair + d, PAIRS)
 
     def p_peer(d):
-        return lax.rem(part + d, TILES)
+        return lax.rem(member + d, MEMBERS)
 
     def c_peer(d):
         return lax.rem(mc + d, CH)
 
+    def lanes(tile):
+        return pl.ds(pl.multiple_of(tile * LANES, LANES), LANES)
+
+    def feat_copy(tile):
+        return pltpu.make_async_copy(feat_in.at[:, :, lanes(tile)], feat.at[:, :, lanes(tile)], in_s.at[tile])
+
+    def cot_copy(tile):
+        return pltpu.make_async_copy(cot_in.at[:, lanes(tile)], cot.at[:, lanes(tile)], in_s.at[TILES + tile])
+
+    sf_copy = pltpu.make_async_copy(sf_in, sf, in_s.at[2 * TILES])
+    lf_copy = pltpu.make_async_copy(lf_in, lf, in_s.at[2 * TILES + 1])
+    sf_copy.start()
+    for tile in range(TILES):
+        feat_copy(tile).start()
+        cot_copy(tile).start()
+    lf_copy.start()
+
     barrier = pltpu.get_barrier_semaphore()
     peers = [(before, mc), (after, mc)]
-    peers += [(plane * TILES + p_peer(d), mc) for d in range(1, TILES)]
+    peers += [(z_peer(d) * MEMBERS + member, mc) for d in range(1, PAIRS)]
+    peers += [(pair * MEMBERS + p_peer(d), mc) for d in range(1, MEMBERS)]
     peers += [(me, c_peer(d)) for d in range(1, CH)]
-    peers += [(z_peer(d) * TILES + part, mc) for d in range(1, PLANES)]
     for peer in peers:
         pl.semaphore_signal(barrier, inc=1, device_id=peer, device_id_type=MESH)
-
-    def lanes(tile):
-        return pl.ds(pl.multiple_of(tile * LANES, LANES), LANES)
 
     def taps(which, tile, start, count):
         total = sf[which, 0:1, lanes(tile)] * xf[tile, which, pl.ds(HEAD + start, count), :]
@@ -79,6 +99,8 @@
         )
 
     def first(tile, _):
+        feat_copy(tile).wait()
+        cot_copy(tile).wait()
         zero8 = jnp.zeros((8, LANES), F32)
         for which in range(3):
             xf[tile, which, pl.ds(HEAD, ROWS), :] = feat[which, :, lanes(tile)].astype(F32)
@@ -99,16 +121,18 @@
         bwd[tile, pl.ds(SPAN, 16), :] = jnp.concatenate(
             [xf[tile, 0, pl.ds(HEAD, 8), :], cotf[:8]], 0
         ).astype(BF16)
-
-        @pl.when(tile == 0)
-        def _():
-            pl.semaphore_wait(barrier, len(peers))
-
+        return 0
+
+    def send(tile, _):
         fwd_copy(tile).start()
         bwd_copy(tile).start()
         return 0
 
+    sf_copy.wait()
     lax.fori_loop(0, TILES, first, 0)
+    pl.semaphore_wait(barrier, len(peers))
+    lax.fori_loop(0, TILES, send, 0)
+    lf_copy.wait()
 
     row = lax.broadcasted_iota(jnp.int32, (SPAN, SPAN), 0)
     col = lax.broadcasted_iota(jnp.int32, (SPAN, SPAN), 1)
@@ -118,17 +142,16 @@
     hrev[1] = jnp.dot(hb, flip, preferred_element_type=F32)
 
     def build(g, _):
-        wide = [
-            jnp.broadcast_to(
-                jnp.concatenate([hrev[i, pl.ds(g, 1), :], jnp.zeros((1, SPAN), F32)], 1), (SPAN, 2 * SPAN)
-            )
-            for i in range(2)
-        ]
-        bmat[g] = pltpu.roll(wide[0], 0, axis=1, stride=1, stride_axis=0).astype(BF16)
-        amat[g] = pltpu.roll(wide[1], 1, axis=1, stride=1, stride_axis=0).astype(BF16)
-        return 0
-
-    lax.fori_loop(0, TILES * PER, build, 0)
+        wide = [jnp.broadcast_to(hrev[i, pl.ds(g, 1), :], (SPAN, SPAN)) for i in range(2)]
+        ahead = pltpu.roll(wide[0], 0, axis=1, stride=1, stride_axis=0)
+        behind = pltpu.roll(wide[1], 1, axis=1, stride=1, stride_axis=0)
+        bmat[g, :, :SPAN] = jnp.where(col >= row, ahead, 0.0).astype(BF16)
+        bmat[g, :, SPAN:] = jnp.where(col < row, ahead, 0.0).astype(BF16)
+        amat[g, :, :SPAN] = jnp.where(col > row, behind, 0.0).astype(BF16)
+        amat[g, :, SPAN:] = jnp.where(col <= row, behind, 0.0).astype(BF16)
+        return 0
+
+    lax.fori_loop(0, TILES * PER, build, 0, unroll=4)
 
     lane = lax.rem(lax.broadcasted_iota(jnp.int32, (1, 2 * LANES), 1), LANES) // GROUP
 
@@ -137,6 +160,11 @@
         for g in range(1, PER):
             total = jnp.where(lane == g, stacked[g * SPAN : (g + 1) * SPAN], total)
         return total[:, :LANES], total[:, LANES:]
+
+    def scat_copy(owner, slot):
+        return remote(
+            rawb.at[owner], scat.at[slot], rs_s.at[owner], rs_r.at[slot], pair * MEMBERS + owner, mc
+        )
 
     def second(tile, _):
         fwd_copy(tile).wait_recv()
@@ -188,25 +216,27 @@
         masked = jnp.concatenate([z_own * (lane == g).astype(BF16) for g in range(PER)], 0)
         gram = lax.dot_general(masked, d_win, (((1,), (1,)), ((), ())), preferred_element_type=F32)
         for g in range(PER):
-            skew = pltpu.roll(
-                gram[g * SPAN : (g + 1) * SPAN], SPAN + 1, axis=1, stride=1, stride_axis=0
-            )
-            rawb[tile, 24 + g : 25 + g, :] = jnp.sum(skew[:, :SPAN], 0, keepdims=True)
+            rows = gram[g * SPAN : (g + 1) * SPAN]
+            both = jnp.where(row + col >= SPAN - 1, rows[:, :SPAN], rows[:, SPAN:])
+            skew = pltpu.roll(both, 1, axis=1, stride=1, stride_axis=0)
+            rawb[TILES + tile, 8 + g : 9 + g, :] = jnp.sum(skew, 0, keepdims=True)
         for which in range(3):
+            at, row0 = which // 2 * TILES + tile, which % 2 * 8
             for j in range(TAPS):
                 prod = dd[tile, which, pl.ds(0, ROWS), :] * xf[tile, which, pl.ds(HEAD - j, ROWS), :]
-                rawb[tile, 8 * which + j : 8 * which + j + 1, :] = jnp.sum(prod, 0, keepdims=True)
-            rawb[tile, 8 * which + 7 : 8 * which + 8, :] = jnp.zeros((1, LANES), F32)
-
-        @pl.when(tile != part)
-        def _():
-            remote(
-                rawb.at[tile], scat.at[part], rs_s.at[tile], rs_r.at[part], plane * TILES + tile, mc
-            ).start()
-
-        @pl.when(tile == part)
-        def _():
-            scat[part] = rawb[tile]
+                rawb[at, row0 + j : row0 + j + 1, :] = jnp.sum(prod, 0, keepdims=True)
+            rawb[at, row0 + 7 : row0 + 8, :] = jnp.zeros((1, LANES), F32)
+
+        for half in range(2):
+            owner = half * TILES + tile
+
+            @pl.when(owner != member)
+            def _():
+                scat_copy(owner, member).start()
+
+            @pl.when(owner == member)
+            def _():
+                scat[member] = rawb[owner]
 
         return 0
 
@@ -235,49 +265,45 @@
     lax.fori_loop(0, 3, adjoint, 0)
 
     def scat_wait(d, _):
-        peer = p_peer(d)
-        remote(rawb.at[peer], scat.at[peer], rs_s.at[peer], rs_r.at[peer], plane * TILES + peer, mc).wait()
-        return 0
-
-    lax.fori_loop(1, TILES, scat_wait, 0)
-    gath[plane] = jnp.sum(scat[...], 0)
+        scat_copy(p_peer(d), p_peer(d)).wait()
+        return 0
+
+    lax.fori_loop(1, MEMBERS, scat_wait, 0)
+    gath[pair] = jnp.sum(scat[...], 0)
 
     def z_copy(peer, slot):
         return remote(
-            gath.at[plane], gath.at[slot], z_s.at[peer], z_r.at[slot], peer * TILES + part, mc
+            gath.at[pair], gath.at[slot], z_s.at[peer], z_r.at[slot], peer * MEMBERS + member, mc
         )
 
     def z_start(d, _):
-        z_copy(z_peer(d), plane).start()
+        z_copy(z_peer(d), pair).start()
         return 0
 
     def z_wait(d, _):
         z_copy(z_peer(d), z_peer(d)).wait()
         return 0
 
-    lax.fori_loop(1, PLANES, z_start, 0)
+    lax.fori_loop(1, PAIRS, z_start, 0)
     lax.fori_loop(3, TILES, adjoint, 0)
-    lax.fori_loop(1, PLANES, z_wait, 0)
-    fin[part] = jnp.sum(gath[...], 0)
+    lax.fori_loop(1, PAIRS, z_wait, 0)
+    fin[member] = jnp.sum(gath[...], 0)
 
     def ag_copy(peer, slot):
-        return remote(fin.at[part], fin.at[slot], ag_s.at[peer], ag_r.at[slot], plane * TILES + peer, mc)
+        return remote(fin.at[member], fin.at[slot], ag_s.at[peer], ag_r.at[slot], pair * MEMBERS + peer, mc)
 
     def ag_start(d, _):
-        ag_copy(p_peer(d), part).start()
+        ag_copy(p_peer(d), member).start()
         return 0
 
     def ag_wait(d, _):
         ag_copy(p_peer(d), p_peer(d)).wait()
         return 0
 
-    lax.fori_loop(1, TILES, ag_start, 0)
-    lax.fori_loop(1, TILES, ag_wait, 0)
-    whole = fin[...].reshape(TILES * 32 // 8, 8, LANES)
-    sq[mc] = jnp.sum(whole * whole, 0)
+    top = pl.ds(0, 1)
 
     def ch_copy(peer, slot):
-        return remote(sq.at[mc], sq.at[slot], ch_s.at[peer], ch_r.at[slot], me, peer)
+        return remote(sq.at[mc, top], sq.at[slot, top], ch_s.at[peer], ch_r.at[slot], me, peer)
 
     def ch_start(d, _):
         ch_copy(c_peer(d), mc).start()
@@ -287,17 +313,41 @@
         ch_copy(c_peer(d), c_peer(d)).wait()
         return 0
 
+    def sq_copy(peer, slot):
+        return remote(
+            part_sq.at[member, top],
+            part_sq.at[slot, top],
+            sq_s.at[peer],
+            sq_r.at[slot],
+            pair * MEMBERS + peer,
+            mc,
+        )
+
+    def sq_start(d, _):
+        sq_copy(p_peer(d), member).start()
+        return 0
+
+    def sq_wait(d, _):
+        sq_copy(p_peer(d), p_peer(d)).wait()
+        return 0
+
+    whole = fin[member]
+    sq[mc, top, :] = jnp.sum(whole * whole, 0, keepdims=True)
     lax.fori_loop(1, CH, ch_start, 0)
+    lax.fori_loop(1, MEMBERS, ag_start, 0)
     lax.fori_loop(1, CH, ch_wait, 0)
-    total = jnp.sum(sq[...], 0)
-    total = jnp.sum(jnp.sum(total, 0, keepdims=True), 1, keepdims=True)
+    part_sq[member, top, :] = jnp.sum(sq[:, 0, :], 0, keepdims=True)
+    lax.fori_loop(1, MEMBERS, sq_start, 0)
+    lax.fori_loop(1, MEMBERS, ag_wait, 0)
+    lax.fori_loop(1, MEMBERS, sq_wait, 0)
+    total = jnp.sum(jnp.sum(part_sq[:, 0, :], 0, keepdims=True), 1, keepdims=True)
     factor = lax.rsqrt(total / COUNT + 1e-06)
     for tile in range(TILES):
         for which in range(3):
             out_short[which, :, tile * LANES : (tile + 1) * LANES] = (
-                fin[tile, 8 * which : 8 * which + TAPS, :] * factor
+                fin[which // 2 * TILES + tile, which % 2 * 8 : which % 2 * 8 + TAPS, :] * factor
             )
-        out_long[8 * tile : 8 * tile + 8, :] = fin[tile, 24:32, :] * factor
+        out_long[8 * tile : 8 * tile + 8, :] = fin[TILES + tile, 8:16, :] * factor
 
     def drain(tile, _):
         fwd_copy(tile).wait_send()
@@ -311,7 +361,8 @@
 
 def on_device(features, short_filter, long_filter, cotangent):
     vmem = pl.BlockSpec(memory_space=pltpu.VMEM)
-    sems = [pltpu.SemaphoreType.DMA((n,)) for n in (8,) * 8 + (12, 12) + (8,) * 5]
+    hbm = pl.BlockSpec(memory_space=pltpu.HBM)
+    sems = [pltpu.SemaphoreType.DMA((n,)) for n in (8,) * 6 + (16, 16, 6, 6, 16, 16, 8, 8, 16, 16, 8, 18)]
     return pl.pallas_call(
         kernel,
         out_shape=(
@@ -319,9 +370,13 @@
             jax.ShapeDtypeStruct((3, TAPS, TILES * LANES), F32),
             jax.ShapeDtypeStruct((TILES * PER, SPAN), F32),
         ),
-        in_specs=[vmem] * 4,
+        in_specs=[hbm] * 4,
         out_specs=(pl.BlockSpec(memory_space=pl.ANY), vmem, vmem),
         scratch_shapes=[
+            pltpu.VMEM((3, ROWS, TILES * LANES), BF16),
+            pltpu.VMEM((3, TAPS, TILES * LANES), F32),
+            pltpu.VMEM((TILES * PER, SPAN), F32),
+            pltpu.VMEM((ROWS, TILES * LANES), BF16),
             pltpu.VMEM((TILES, 3, HEAD + ROWS + 8, LANES), F32),
             pltpu.VMEM((TILES, ROWS, LANES), F32),
             pltpu.VMEM((TILES, ROWS, LANES), F32),
@@ -334,17 +389,18 @@
             pltpu.VMEM((TILES * PER, SPAN, 2 * SPAN), BF16),
             pltpu.VMEM((2, TILES * PER, SPAN), F32),
             pltpu.VMEM((3, ROWS, TILES * LANES), BF16),
-            pltpu.VMEM((TILES, 32, LANES), F32),
-            pltpu.VMEM((TILES, 32, LANES), F32),
-            pltpu.VMEM((PLANES, 32, LANES), F32),
-            pltpu.VMEM((TILES, 32, LANES), F32),
+            pltpu.VMEM((MEMBERS, 16, LANES), F32),
+            pltpu.VMEM((MEMBERS, 16, LANES), F32),
+            pltpu.VMEM((PAIRS, 16, LANES), F32),
+            pltpu.VMEM((MEMBERS, 16, LANES), F32),
             pltpu.VMEM((CH, 8, LANES), F32),
+            pltpu.VMEM((MEMBERS, 8, LANES), F32),
             *sems,
         ],
         compiler_params=pltpu.CompilerParams(
             collective_id=0, has_side_effects=True, vmem_limit_bytes=48 * 1024 * 1024
         ),
-    )(features, short_filter, long_filter, cotangent)
+    )(*(pltpu.with_memory_space_constraint(x, pltpu.HBM) for x in (features, short_filter, long_filter, cotangent)))
 
 
 def solution(mesh):

time: 69.3 us -> 59.8 us (0.86)
  Pallas kernels: 61.8 us -> 56.6 us
  local copies, waits for them, and re-layouts: 6.49 us -> 2.4 us
    pallas_call x1, Pallas kernels: 61.8 us -> 56.6 us  [on_device(): pl.pallas_call(kernel, out_shape=(jax.ShapeDtypeStruct((3, ROWS, TILES *...]
    unnamed x11 -> x3, local copies, waits for them, and re-layouts: 6.49 us -> 2.4 us
where the time goes in v2:
time: 59.8 us; the launch traced here: 59.7 us
  Pallas kernels  56.6 us (95%)
  local copies, waits for them, and re-layouts  2.4 us (4%)
  between operations  0.64 us (1%)
    pallas_call x1, Pallas kernels, on_device(): pl.pallas_call(kernel, out_shape=(jax.ShapeDtypeStruct((3, ROWS, TILES *...  56.6 us
    unnamed x3, local copies, waits for them, and re-layouts  2.4 us

profile of v2, /device:TPU:1, one launch (start us, length us, event | category | flops | bytes accessed | tf_op | source)
XLA Modules:
  0.0 59.7 jit_solution(7566914262625534658)
XLA Ops:
  0.6 56.6 %shard_map.67 = (bf16[3,256,1024]{2,1,0:T(8,128)(2,1)S(1)}, f32[3,7,1024]{2,1,0:T(8,128)S(1)}, f32[64,128]{1,0:T(8,128)S(1)}) custom-call(bf16[3,256,1024]{2,1,0:T(8,128)(2,1)} %feat_in.1, f32[3,7,1024]{2,1,0:T(8,128)} %sf_in.1, f32[64,128]{1,0:T(8,128)} %lf_in.1, bf16[256,1024]{1,0:T(8,128)(2,1)} %cot_in.1), custom_call_target="tpu_custom_call" | custom-call | tf_op jit(solution)/shard_map/pallas_call | solution.py:366
  57.3 1.1 %copy.10 = bf16[3,256,1024]{2,1,0:T(8,128)(2,1)} copy(bf16[3,256,1024]{2,1,0:T(8,128)(2,1)S(1)} %get-tuple-element.6) | data formatting | bytes 3145728
  58.4 0.6 %copy.11 = f32[3,7,1024]{2,1,0:T(8,128)} copy(f32[3,7,1024]{2,1,0:T(8,128)S(1)} %get-tuple-element.7) | data formatting | bytes 172032
  59.1 0.6 %copy.12 = f32[64,128]{1,0:T(8,128)} copy(f32[64,128]{1,0:T(8,128)S(1)} %get-tuple-element.8) | data formatting | bytes 65536

commit v3 on v2

--- a/solution.py
+++ b/solution.py
@@ -268,7 +268,7 @@
         scat_copy(p_peer(d), p_peer(d)).wait()
         return 0
 
-    lax.fori_loop(1, MEMBERS, scat_wait, 0)
+    lax.fori_loop(1, MEMBERS, scat_wait, 0, unroll=True)
     gath[pair] = jnp.sum(scat[...], 0)
 
     def z_copy(peer, slot):
@@ -284,9 +284,9 @@
         z_copy(z_peer(d), z_peer(d)).wait()
         return 0
 
-    lax.fori_loop(1, PAIRS, z_start, 0)
+    lax.fori_loop(1, PAIRS, z_start, 0, unroll=True)
     lax.fori_loop(3, TILES, adjoint, 0)
-    lax.fori_loop(1, PAIRS, z_wait, 0)
+    lax.fori_loop(1, PAIRS, z_wait, 0, unroll=True)
     fin[member] = jnp.sum(gath[...], 0)
 
     def ag_copy(peer, slot):
@@ -333,13 +333,13 @@
 
     whole = fin[member]
     sq[mc, top, :] = jnp.sum(whole * whole, 0, keepdims=True)
-    lax.fori_loop(1, CH, ch_start, 0)
-    lax.fori_loop(1, MEMBERS, ag_start, 0)
-    lax.fori_loop(1, CH, ch_wait, 0)
+    lax.fori_loop(1, CH, ch_start, 0, unroll=True)
+    lax.fori_loop(1, MEMBERS, ag_start, 0, unroll=True)
+    lax.fori_loop(1, CH, ch_wait, 0, unroll=True)
     part_sq[member, top, :] = jnp.sum(sq[:, 0, :], 0, keepdims=True)
-    lax.fori_loop(1, MEMBERS, sq_start, 0)
+    lax.fori_loop(1, MEMBERS, sq_start, 0, unroll=True)
     lax.fori_loop(1, MEMBERS, ag_wait, 0)
-    lax.fori_loop(1, MEMBERS, sq_wait, 0)
+    lax.fori_loop(1, MEMBERS, sq_wait, 0, unroll=True)
     total = jnp.sum(jnp.sum(part_sq[:, 0, :], 0, keepdims=True), 1, keepdims=True)
     factor = lax.rsqrt(total / COUNT + 1e-06)
     for tile in range(TILES):

time: 59.8 us -> 59.8 us (level)
  no operation moved by 1% of the time
where the time goes in v3:
time: 59.8 us; the launch traced here: 59.6 us
  Pallas kernels  56.6 us (95%)
  local copies, waits for them, and re-layouts  2.4 us (4%)
  between operations  0.64 us (1%)
    pallas_call x1, Pallas kernels, on_device(): pl.pallas_call(kernel, out_shape=(jax.ShapeDtypeStruct((3, ROWS, TILES *...  56.6 us
    unnamed x3, local copies, waits for them, and re-layouts  2.4 us

profile of v3, /device:TPU:1, one launch (start us, length us, event | category | flops | bytes accessed | tf_op | source)
XLA Modules:
  0.0 59.6 jit_solution(12924279727897849876)
XLA Ops:
  0.6 56.6 %shard_map.67 = (bf16[3,256,1024]{2,1,0:T(8,128)(2,1)S(1)}, f32[3,7,1024]{2,1,0:T(8,128)S(1)}, f32[64,128]{1,0:T(8,128)S(1)}) custom-call(bf16[3,256,1024]{2,1,0:T(8,128)(2,1)} %feat_in.1, f32[3,7,1024]{2,1,0:T(8,128)} %sf_in.1, f32[64,128]{1,0:T(8,128)} %lf_in.1, bf16[256,1024]{1,0:T(8,128)(2,1)} %cot_in.1), custom_call_target="tpu_custom_call" | custom-call | tf_op jit(solution)/shard_map/pallas_call | solution.py:366
  57.2 1.1 %copy.10 = bf16[3,256,1024]{2,1,0:T(8,128)(2,1)} copy(bf16[3,256,1024]{2,1,0:T(8,128)(2,1)S(1)} %get-tuple-element.6) | data formatting | bytes 3145728
  58.4 0.6 %copy.11 = f32[3,7,1024]{2,1,0:T(8,128)} copy(f32[3,7,1024]{2,1,0:T(8,128)S(1)} %get-tuple-element.7) | data formatting | bytes 172032
  59.0 0.6 %copy.12 = f32[64,128]{1,0:T(8,128)} copy(f32[64,128]{1,0:T(8,128)S(1)} %get-tuple-element.8) | data formatting | bytes 65536
